TPU v7x, 32 devices: a whole 2x2x4 slice. The times are simulated.
32 devices in a mesh: inline: 4 (over y, core), xline: 8 (over z, x).
Axes of the slice: x: 2, y: 2, z: 4, core: 2. Of those that a mesh axis runs over, the one named last changes fastest.
Arguments:
- queries: bfloat16 [4, 8, 2, 64, 1024], P('inline', 'xline'), may hold values from -6 to 6
- keys: bfloat16 [4, 8, 2, 64, 1024], P('inline', 'xline'), may hold values from -6 to 6
- values: bfloat16 [4, 8, 2, 64, 1024], P('inline', 'xline'), may hold values from -6 to 6
- grad_out: bfloat16 [4, 8, 2, 64, 1024], P('inline', 'xline'), may hold values from -6 to 6
Outputs:
- grad_q: bfloat16 [4, 8, 2, 64, 1024], P('inline', 'xline')
- grad_k: bfloat16 [4, 8, 2, 64, 1024], P('inline', 'xline')
- grad_v: bfloat16 [4, 8, 2, 64, 1024], P('inline', 'xline')
All inputs are finite; a program needn't handle non-finite values.
Results may differ from a plain program's by a relative error of at most 0.012.
Values may be sent and summed in bfloat16 or wider, within the bound.
A program may use at most 128 MiB of HBM per device.

v0:
```python
import math

import jax
import jax.numpy as jnp
import numpy as np
from jax import lax
from jax.sharding import PartitionSpec as P

HD = 64


NEG_FILL = -1e30


def with_halo(x, sides, width):
    for axis, dim in sides:
        peers, length = (lax.axis_size(axis), x.shape[dim])
        up = [(i, (i + 1) % peers) for i in range(peers - 1)]
        down = [(j, i) for i, j in up]
        last = lax.slice_in_dim(x, length - width, length, axis=dim)
        first = lax.slice_in_dim(x, 0, width, axis=dim)
        before = lax.ppermute(last, axis, up)
        after = lax.ppermute(first, axis, down)
        x = jnp.concatenate([before, x, after], axis=dim)
    return x


def full_pairs():
    return [(shift_x, shift_y) for shift_x in range(3) for shift_y in range(3)]


def tile_grads(query_rows, grad_rows, key_win, value_win, inside):
    scaling = 1.0 / math.sqrt(query_rows.shape[-1])
    scores = (
        jnp.einsum("nqd,nkd->nqk", query_rows, key_win, preferred_element_type=jnp.float32)
        * scaling
    )
    scores = jnp.where(inside, scores, NEG_FILL)
    row_max = jnp.max(scores, axis=-1)
    row_total = jnp.sum(jnp.exp(scores - row_max[..., None]), axis=-1)
    log_norm = row_max + jnp.log(row_total)
    weights = jnp.exp(scores - log_norm[..., None])
    weights_low = weights.astype(jnp.bfloat16)
    attended = jnp.einsum(
        "nqk,nkd->nqd", weights_low, value_win, preferred_element_type=jnp.float32
    )
    row_dot = jnp.sum(grad_rows.astype(jnp.float32) * attended, axis=-1)
    dprobs = jnp.einsum("nqd,nkd->nqk", grad_rows, value_win, preferred_element_type=jnp.float32)
    dscores = (weights * (dprobs - row_dot[..., None])).astype(jnp.bfloat16)
    grad_query = (
        jnp.einsum("nqk,nkd->nqd", dscores, key_win, preferred_element_type=jnp.float32) * scaling
    )
    grad_key = (
        jnp.einsum("nqk,nqd->nkd", dscores, query_rows, preferred_element_type=jnp.float32)
        * scaling
    )
    grad_value = jnp.einsum(
        "nqk,nqd->nkd", weights_low, grad_rows, preferred_element_type=jnp.float32
    )
    return (grad_query, grad_key, grad_value, log_norm, row_dot)


def sweep_tiles(query_h, grad_h, padded_kv, totals, first_ext, pairs, base_y, tiles_y):
    heads_here, tiles_x, rows_q, tiles_z, tile_len, head_dim = query_h.shape
    rows_k = padded_kv.shape[3]
    block_x = 1
    while block_x * heads_here * rows_q * tiles_z * tile_len < 512 and tiles_x % (2 * block_x) == 0:
        block_x = block_x * 2
    query_tiles = heads_here * block_x * rows_q * tiles_z
    count_pairs = len(pairs)
    depth_z = min(3, tiles_z)
    starts = [min(max(tile_c - 1, 0), tiles_z - depth_z) for tile_c in range(tiles_z)]
    z_index = np.array(
        [[starts[tile_c] + slot for slot in range(depth_z)] for tile_c in range(tiles_z)], np.int32
    )
    z_valid = np.abs(z_index - np.arange(tiles_z)[:, None]) <= 1
    selector = np.zeros((3, tiles_z, depth_z), np.float32)
    for offset_z in range(3):
        for tile_c in range(tiles_z):
            for slot in range(depth_z):
                if z_index[tile_c, slot] == tile_c + offset_z - 1:
                    selector[offset_z, tile_c, slot] = 1.0
    selector = jnp.array(selector)
    flat_z = jnp.array(z_index.reshape(-1))
    count_slots = count_pairs * depth_z
    pair_table = jnp.array(pairs, jnp.int32)
    grid_y = base_y + first_ext - 1 + jnp.arange(rows_q, dtype=jnp.int32)[:, None, None]
    key_y = grid_y + pair_table[:, 1] - 1
    y_inside = (grid_y >= 0) & (grid_y < tiles_y) & (key_y >= 0) & (key_y < tiles_y)
    fixed_inside = y_inside[..., None] & jnp.array(z_valid)[None, :, None, :]

    def sweep_step(totals, block_index):
        first_x = block_index * block_x
        key_x = (
            first_x
            + jnp.arange(block_x, dtype=jnp.int32)[:, None, None, None, None]
            + pair_table[:, 0][None, None, None, :, None]
            - 1
        )
        inside = (key_x >= 0) & (key_x < tiles_x) & fixed_inside[None]
        inside = jnp.broadcast_to(
            inside[None, ..., None],
            (heads_here, block_x, rows_q, tiles_z, count_pairs, depth_z, tile_len),
        )
        inside = inside.reshape(query_tiles, 1, count_slots * tile_len)
        key_slab = lax.dynamic_slice_in_dim(padded_kv, first_x, block_x + 2, 2)
        pieces = []
        for shift_x, shift_y in pairs:
            plane = key_slab[
                :,
                :,
                shift_x : shift_x + block_x,
                first_ext + shift_y - 1 : first_ext + shift_y - 1 + rows_q,
            ]
            chosen = jnp.take(plane, flat_z, axis=4)
            pieces.append(
                chosen.reshape(2, heads_here, block_x, rows_q, tiles_z, depth_z, tile_len, head_dim)
            )
        windows = jnp.stack(pieces, axis=5)
        windows = windows.reshape(2, query_tiles, count_slots * tile_len, head_dim)
        query_rows = lax.dynamic_slice_in_dim(query_h, first_x, block_x, 1).reshape(
            query_tiles, tile_len, head_dim
        )
        grad_rows = lax.dynamic_slice_in_dim(grad_h, first_x, block_x, 1).reshape(
            query_tiles, tile_len, head_dim
        )
        grad_query, grad_key, grad_value, log_norm, row_dot = tile_grads(
            query_rows, grad_rows, windows[0], windows[1], inside
        )
        deposits = jnp.stack([grad_key, grad_value]).reshape(
            2, heads_here, block_x, rows_q, tiles_z, count_pairs, depth_z, tile_len, head_dim
        )
        by_offset = jnp.einsum(
            "abxyzpstf,wzs->wabxyzptf", deposits, selector, precision=lax.Precision.HIGHEST
        )
        deposit = jnp.zeros(
            (2, heads_here, block_x + 2, rows_k, tiles_z + 2, tile_len, head_dim), jnp.float32
        )
        for pair_index, (shift_x, shift_y) in enumerate(pairs):
            for offset_z in range(3):
                deposit = deposit.at[
                    :,
                    :,
                    shift_x : shift_x + block_x,
                    first_ext + shift_y - 1 : first_ext + shift_y - 1 + rows_q,
                    offset_z : offset_z + tiles_z,
                ].add(by_offset[offset_z, :, :, :, :, :, pair_index])
        current = (
            lax.dynamic_slice_in_dim(totals, first_x, block_x + 2, 2)
            + deposit[:, :, :, :, 1 : tiles_z + 1]
        )
        totals = lax.dynamic_update_slice_in_dim(totals, current, first_x, 2)
        row_shape = (heads_here, block_x, rows_q, tiles_z, tile_len)
        return (
            totals,
            (
                grad_query.astype(jnp.bfloat16).reshape(row_shape + (head_dim,)),
                log_norm.reshape(row_shape),
                row_dot.reshape(row_shape),
            ),
        )

    totals, outputs = lax.scan(sweep_step, totals, jnp.arange(tiles_x // block_x, dtype=jnp.int32))

    def regroup(array):
        moved = jnp.moveaxis(array, 0, 1)
        return moved.reshape((heads_here, tiles_x) + moved.shape[3:])

    return (totals, regroup(outputs[0]), regroup(outputs[1]), regroup(outputs[2]))


def shards(queries, keys, values, grad_out):
    query_tok, key_tok, value_tok, grad_tok = (
        lax.all_to_all(queries, "inline", split_axis=4, concat_axis=0, tiled=True),
        lax.all_to_all(keys, "inline", split_axis=4, concat_axis=0, tiled=True),
        lax.all_to_all(values, "inline", split_axis=4, concat_axis=0, tiled=True),
        lax.all_to_all(grad_out, "inline", split_axis=4, concat_axis=0, tiled=True),
    )
    tiles_x, rows_y, tiles_z, tile_len, width = query_tok.shape
    heads_here = width // HD
    base_y = lax.axis_index("xline") * rows_y
    tiles_y = rows_y * lax.axis_size("xline")

    def split_heads(array):
        return array.reshape(tiles_x, rows_y, tiles_z, tile_len, heads_here, HD).transpose(
            4, 0, 1, 2, 3, 5
        )

    pair = jnp.stack([split_heads(key_tok), split_heads(value_tok)])
    kv_ext = with_halo(pair, (("xline", 3),), 1)
    query_heads = split_heads(query_tok)
    grad_heads = split_heads(grad_tok)
    padded_kv = jnp.pad(kv_ext, ((0, 0), (0, 0), (1, 1), (0, 0), (0, 0), (0, 0), (0, 0)))
    totals = jnp.zeros((2, heads_here, tiles_x + 2, rows_y + 2, tiles_z, tile_len, HD), jnp.float32)
    totals, grad_query, log_norm, row_dot = sweep_tiles(
        query_heads, grad_heads, padded_kv, totals, 1, full_pairs(), base_y, tiles_y
    )
    folded = with_halo(totals[:, :, 1 : tiles_x + 1], (("xline", 3),), 1)
    own_grads = folded[:, :, :, 2 : rows_y + 2]
    own_grads = own_grads.at[:, :, :, 0].add(folded[:, :, :, 0])
    own_grads = own_grads.at[:, :, :, rows_y - 1].add(folded[:, :, :, rows_y + 3])
    key_value_grads = own_grads.astype(jnp.bfloat16)

    def to_tokens(array):
        return array.transpose(1, 2, 3, 4, 0, 5).reshape(tiles_x, rows_y, tiles_z, tile_len, width)

    grad_query_tok, grad_key_tok, grad_value_tok = (
        lax.all_to_all(to_tokens(grad_query), "inline", split_axis=0, concat_axis=4, tiled=True),
        lax.all_to_all(
            to_tokens(key_value_grads[0]), "inline", split_axis=0, concat_axis=4, tiled=True
        ),
        lax.all_to_all(
            to_tokens(key_value_grads[1]), "inline", split_axis=0, concat_axis=4, tiled=True
        ),
    )
    return (grad_query_tok, grad_key_tok, grad_value_tok)


def solution(mesh):
    placed = (
        P("inline", "xline", None, None, None),
        P("inline", "xline", None, None, None),
        P("inline", "xline", None, None, None),
        P("inline", "xline", None, None, None),
    )
    return jax.shard_map(
        shards,
        mesh=mesh,
        in_specs=placed,
        out_specs=(
            P("inline", "xline", None, None, None),
            P("inline", "xline", None, None, None),
            P("inline", "xline", None, None, None),
        ),
        check_vma=False,
    )
```

profile of v0, /device:TPU:0, one launch (start us, length us, event | category | flops | bytes accessed | tf_op | source)
XLA Modules:
  0.0 860.7 jit_solution(14491774503227842536)
XLA Ops:
  26.9 5.7 collective-permute-start
  53.8 21.6 %collective-permute-done = bf16[2,4,4,1,2,64,64]{6,1,5,4,2,3,0:T(4,128)(2,1)} collective-permute-done((bf16[2,4,4,1,2,64,64]{6,1,5,4,2,3,0:T(4,128)(2,1)}, bf16[2,4,4,1,2,64,64]{6,1,5,4,2,3,0:T(4,128)(2,1)}, u32[]{:S(2)}, u32[]{:S(2)}) %collective-permute-start) | collective-permute-done | bytes 524320 | tf_op jit(solution)/shard_map/ppermute | solution.py:22
  85.9 650.9 %while.46 = (s32[]{:T(128)}, f32[2,4,6,3,2,64,64]{6,5,1,0,4,3,2:T(8,128)}, bf16[4,4,1,1,2,64,64]{6,5,4,1,3,2,0:T(8,128)(2,1)}, s32[4]{0:T(128)S(1)}, bf16[4,4,1,...) while((s32[]{:T(128)}, ...), condition=%wide.region_4.6_spmd.clone.clone, body=%wide.region_0.5_spmd.sunk.clone.clone.sunk | while | flops 507347008 | bytes 234356512 | solution.py:163
  126.9 5.6 fusion.127
  150.3 9.5 %copy.308 = f32[1,4,1,1,2,9,2,64,64]{8,6,7,5,1,0,4,3,2:T(2,128)} copy(f32[1,4,1,1,2,9,2,64,64]{7,6,5,8,4,1,3,2,0:T(2,128)} %stack.43) | data formatting | bytes 4718592 | tf_op jit(solution)/shard_map/while/body/eval_jaxpr/stack | solution.py:130
  164.0 9.4 %copy.307 = f32[1,4,1,1,2,9,2,64,64]{8,6,7,5,1,0,4,3,2:T(2,128)} copy(f32[1,4,1,1,2,9,2,64,64]{7,6,5,8,4,1,3,2,0:T(2,128)} %stack.42) | data formatting | bytes 4718592 | tf_op jit(solution)/shard_map/while/body/eval_jaxpr/stack | solution.py:130
  173.4 43.9 %fusion.132 = f32[3,2,4,1,1,2,9,64,64]{8,0,7,6,2,1,5,4,3:T(4,128)S(1)} fusion(f32[3,2,2,1,1,1,1]{0,2,6,5,4,3,1:T(2,128)S(1)} %get-tuple-element.974, f32[1,4,1,1,2,9,2,64,64]{8,6,7,5,1,0,4,3,2:T(2,128)} %copy.307, f32[1,4,1,1,2,9,2,64,64]{8,6,7,5,1,0,4,3,2:T(2,128)} %copy.308), kind=kOutput, calls=%fused_computation.14.clone.2 | convolution fusion | flops 43646976 | bytes 11796528 | tf_op jit(solution)/shard_map/while/body/eval_jaxpr/abxyzpstf,wzs->wabxyzptf/dot_general | solution.py:133
  222.0 11.5 %fusion.140 = (f32[1,2,4,1,1,2,1,64,64]{8,0,7,6,2,1,5,4,3:T(1,128)S(1)}, f32[1,2,4,1,1,2,1,64,64]{8,0,7,6,2,1,5,4,3:T(1,128)S(1)}, f32[1,2,4,1,1,2,1,64,64]{8,0,...) fusion(f32[3,2,4,1,1,2,9,64,64]{8,0,7,6,2,1,5,4,3:T(4,128)S(1)}, ...), kind=kLoop, calls=%fused_computation.130.clone.1 | loop fusion | bytes 9961472 | tf_op jit(solution)/shard_map/while/body/eval_jaxpr/slice | solution.py:147
  288.9 5.6 fusion.127
  312.0 9.5 %copy.308 = f32[1,4,1,1,2,9,2,64,64]{8,6,7,5,1,0,4,3,2:T(2,128)} copy(f32[1,4,1,1,2,9,2,64,64]{7,6,5,8,4,1,3,2,0:T(2,128)} %stack.43) | data formatting | bytes 4718592 | tf_op jit(solution)/shard_map/while/body/eval_jaxpr/stack | solution.py:130
  325.7 9.4 %copy.307 = f32[1,4,1,1,2,9,2,64,64]{8,6,7,5,1,0,4,3,2:T(2,128)} copy(f32[1,4,1,1,2,9,2,64,64]{7,6,5,8,4,1,3,2,0:T(2,128)} %stack.42) | data formatting | bytes 4718592 | tf_op jit(solution)/shard_map/while/body/eval_jaxpr/stack | solution.py:130
  335.1 43.9 %fusion.132 = f32[3,2,4,1,1,2,9,64,64]{8,0,7,6,2,1,5,4,3:T(4,128)S(1)} fusion(f32[3,2,2,1,1,1,1]{0,2,6,5,4,3,1:T(2,128)S(1)} %get-tuple-element.974, f32[1,4,1,1,2,9,2,64,64]{8,6,7,5,1,0,4,3,2:T(2,128)} %copy.307, f32[1,4,1,1,2,9,2,64,64]{8,6,7,5,1,0,4,3,2:T(2,128)} %copy.308), kind=kOutput, calls=%fused_computation.14.clone.2 | convolution fusion | flops 43646976 | bytes 11796528 | tf_op jit(solution)/shard_map/while/body/eval_jaxpr/abxyzpstf,wzs->wabxyzptf/dot_general | solution.py:133
  383.7 11.5 %fusion.140 = (f32[1,2,4,1,1,2,1,64,64]{8,0,7,6,2,1,5,4,3:T(1,128)S(1)}, f32[1,2,4,1,1,2,1,64,64]{8,0,7,6,2,1,5,4,3:T(1,128)S(1)}, f32[1,2,4,1,1,2,1,64,64]{8,0,...) fusion(f32[3,2,4,1,1,2,9,64,64]{8,0,7,6,2,1,5,4,3:T(4,128)S(1)}, ...), kind=kLoop, calls=%fused_computation.130.clone.1 | loop fusion | bytes 9961472 | tf_op jit(solution)/shard_map/while/body/eval_jaxpr/slice | solution.py:147
  450.6 5.6 fusion.127
  473.8 9.5 %copy.308 = f32[1,4,1,1,2,9,2,64,64]{8,6,7,5,1,0,4,3,2:T(2,128)} copy(f32[1,4,1,1,2,9,2,64,64]{7,6,5,8,4,1,3,2,0:T(2,128)} %stack.43) | data formatting | bytes 4718592 | tf_op jit(solution)/shard_map/while/body/eval_jaxpr/stack | solution.py:130
  487.5 9.4 %copy.307 = f32[1,4,1,1,2,9,2,64,64]{8,6,7,5,1,0,4,3,2:T(2,128)} copy(f32[1,4,1,1,2,9,2,64,64]{7,6,5,8,4,1,3,2,0:T(2,128)} %stack.42) | data formatting | bytes 4718592 | tf_op jit(solution)/shard_map/while/body/eval_jaxpr/stack | solution.py:130
  496.8 43.9 %fusion.132 = f32[3,2,4,1,1,2,9,64,64]{8,0,7,6,2,1,5,4,3:T(4,128)S(1)} fusion(f32[3,2,2,1,1,1,1]{0,2,6,5,4,3,1:T(2,128)S(1)} %get-tuple-element.974, f32[1,4,1,1,2,9,2,64,64]{8,6,7,5,1,0,4,3,2:T(2,128)} %copy.307, f32[1,4,1,1,2,9,2,64,64]{8,6,7,5,1,0,4,3,2:T(2,128)} %copy.308), kind=kOutput, calls=%fused_computation.14.clone.2 | convolution fusion | flops 43646976 | bytes 11796528 | tf_op jit(solution)/shard_map/while/body/eval_jaxpr/abxyzpstf,wzs->wabxyzptf/dot_general | solution.py:133
  545.7 11.5 %fusion.140 = (f32[1,2,4,1,1,2,1,64,64]{8,0,7,6,2,1,5,4,3:T(1,128)S(1)}, f32[1,2,4,1,1,2,1,64,64]{8,0,7,6,2,1,5,4,3:T(1,128)S(1)}, f32[1,2,4,1,1,2,1,64,64]{8,0,...) fusion(f32[3,2,4,1,1,2,9,64,64]{8,0,7,6,2,1,5,4,3:T(4,128)S(1)}, ...), kind=kLoop, calls=%fused_computation.130.clone.1 | loop fusion | bytes 9961472 | tf_op jit(solution)/shard_map/while/body/eval_jaxpr/slice | solution.py:147
  612.4 5.6 fusion.127
  635.7 9.5 %copy.308 = f32[1,4,1,1,2,9,2,64,64]{8,6,7,5,1,0,4,3,2:T(2,128)} copy(f32[1,4,1,1,2,9,2,64,64]{7,6,5,8,4,1,3,2,0:T(2,128)} %stack.43) | data formatting | bytes 4718592 | tf_op jit(solution)/shard_map/while/body/eval_jaxpr/stack | solution.py:130
  649.4 9.4 %copy.307 = f32[1,4,1,1,2,9,2,64,64]{8,6,7,5,1,0,4,3,2:T(2,128)} copy(f32[1,4,1,1,2,9,2,64,64]{7,6,5,8,4,1,3,2,0:T(2,128)} %stack.42) | data formatting | bytes 4718592 | tf_op jit(solution)/shard_map/while/body/eval_jaxpr/stack | solution.py:130
  658.7 43.9 %fusion.132 = f32[3,2,4,1,1,2,9,64,64]{8,0,7,6,2,1,5,4,3:T(4,128)S(1)} fusion(f32[3,2,2,1,1,1,1]{0,2,6,5,4,3,1:T(2,128)S(1)} %get-tuple-element.974, f32[1,4,1,1,2,9,2,64,64]{8,6,7,5,1,0,4,3,2:T(2,128)} %copy.307, f32[1,4,1,1,2,9,2,64,64]{8,6,7,5,1,0,4,3,2:T(2,128)} %copy.308), kind=kOutput, calls=%fused_computation.14.clone.2 | convolution fusion | flops 43646976 | bytes 11796528 | tf_op jit(solution)/shard_map/while/body/eval_jaxpr/abxyzpstf,wzs->wabxyzptf/dot_general | solution.py:133
  707.4 11.5 %fusion.140 = (f32[1,2,4,1,1,2,1,64,64]{8,0,7,6,2,1,5,4,3:T(1,128)S(1)}, f32[1,2,4,1,1,2,1,64,64]{8,0,7,6,2,1,5,4,3:T(1,128)S(1)}, f32[1,2,4,1,1,2,1,64,64]{8,0,...) fusion(f32[3,2,4,1,1,2,9,64,64]{8,0,7,6,2,1,5,4,3:T(4,128)S(1)}, ...), kind=kLoop, calls=%fused_computation.130.clone.1 | loop fusion | bytes 9961472 | tf_op jit(solution)/shard_map/while/body/eval_jaxpr/slice | solution.py:147
  753.4 83.0 %collective-permute-done.2 = f32[2,4,4,1,2,64,64]{6,5,1,0,4,3,2:T(8,128)S(1)} collective-permute-done((f32[2,4,4,1,2,64,64]{6,5,1,0,4,3,2:T(8,128)}, f32[2,4,4,1,2,64,64]{6,5,1,0,4,3,2:T(8,128)S(1)}, u32[]{:S(2)}, u32[]{:S(2)}) %collective-permute-start.2) | collective-permute-done | bytes 1048608 | tf_op jit(solution)/shard_map/ppermute | solution.py:22
  (621 shorter events, 408.6 us)
Async XLA Ops:
  3.0 29.6 %copy-start.17 = (bf16[1,1,2,64,1024]{4,3,2,1,0:T(8,128)(2,1)S(1)}, bf16[1,1,2,64,1024]{4,3,2,1,0:T(8,128)(2,1)}, u32[]{:S(2)}) copy-start(bf16[1,1,2,64,1024]{4,3,2,1,0:T(8,128)(2,1)} %param.70) | copy-start | bytes 786436
  3.0 10.4 %all-to-all-start.1 = ((bf16[4,2,16384]{2,1,0:T(2,128)(2,1)}), bf16[4,2,16384]{2,1,0:T(2,128)(2,1)S(1)}, u32[]{:S(2)}, u32[]{:S(2)}) async-start(bf16[4,2,16384]{2,1,0:T(2,128)(2,1)} %reshape.2396), calls=%async_computation.1 | async-start | bytes 524288 | tf_op jit(solution)/shard_map/all_to_all | solution.py:175
  9.7 27.7 %copy-start.18 = (bf16[1,1,2,64,1024]{4,3,2,1,0:T(8,128)(2,1)S(1)}, bf16[1,1,2,64,1024]{4,3,2,1,0:T(8,128)(2,1)}, u32[]{:S(2)}) copy-start(bf16[1,1,2,64,1024]{4,3,2,1,0:T(8,128)(2,1)} %param.73) | copy-start | bytes 786436
  13.4 9.4 %all-to-all-start.2 = ((bf16[4,2,16384]{2,1,0:T(2,128)(2,1)}), bf16[4,2,16384]{2,1,0:T(2,128)(2,1)S(1)}, u32[]{:S(2)}, u32[]{:S(2)}) async-start(bf16[4,2,16384]{2,1,0:T(2,128)(2,1)} %reshape.2394), calls=%async_computation.2 | async-start | bytes 524288 | tf_op jit(solution)/shard_map/all_to_all | solution.py:176
  17.5 29.4 %copy-start.26 = (s32[9,1]{0,1:T(1,128)S(1)}, s32[9,1]{0,1:T(1,128)}, u32[]{:S(2)}) copy-start(s32[9,1]{0,1:T(1,128)} %constant.1147) | copy-start | bytes 112
  25.6 28.2 %collective-permute-start.1 = (bf16[2,4,4,1,2,64,64]{6,1,5,4,2,3,0:T(4,128)(2,1)}, bf16[2,4,4,1,2,64,64]{6,1,5,4,2,3,0:T(4,128)(2,1)S(1)}, u32[]{:S(2)}, u32[]{:S(2)}) collective-permute-start(bf16[2,4,4,1,2,64,64]{6,1,5,4,2,3,0:T(4,128)(2,1)} %pad_maximum_fusion), channel_id=1, source_target_pairs={{1,0},{2,1},{3,2},{4,3},{5,4},{6,5},{7,6},{9,8},{10,9},{11,10},{12... | collective-permute-start | bytes 1572872 | tf_op jit(solution)/shard_map/ppermute | solution.py:23
  26.9 48.6 %collective-permute-start = (bf16[2,4,4,1,2,64,64]{6,1,5,4,2,3,0:T(4,128)(2,1)}, bf16[2,4,4,1,2,64,64]{6,1,5,4,2,3,0:T(4,128)(2,1)}, u32[]{:S(2)}, u32[]{:S(2)}) collective-permute-start(bf16[2,4,4,1,2,64,64]{6,1,5,4,2,3,0:T(4,128)(2,1)} %pad_maximum_fusion), channel_id=1, source_target_pairs={{0,1},{1,2},{2,3},{3,4},{4,5},{5,6},{6,7},{8,9},{9,10},{10,11},{11... | collective-permute-start | bytes 1572872 | tf_op jit(solution)/shard_map/ppermute | solution.py:22
  34.1 9.4 %all-to-all-start = ((bf16[4,2,16384]{2,1,0:T(2,128)(2,1)}), bf16[4,2,16384]{2,1,0:T(2,128)(2,1)S(1)}, u32[]{:S(2)}, u32[]{:S(2)}) async-start(bf16[4,2,16384]{2,1,0:T(2,128)(2,1)} %reshape.2392), calls=%async_computation | async-start | bytes 524288 | tf_op jit(solution)/shard_map/all_to_all | solution.py:174
  43.5 9.4 %all-to-all-start.3 = ((bf16[4,2,16384]{2,1,0:T(2,128)(2,1)}), bf16[4,2,16384]{2,1,0:T(2,128)(2,1)S(1)}, u32[]{:S(2)}, u32[]{:S(2)}) async-start(bf16[4,2,16384]{2,1,0:T(2,128)(2,1)} %reshape.2398), calls=%async_computation.3 | async-start | bytes 524288 | tf_op jit(solution)/shard_map/all_to_all | solution.py:177
  86.2 7.0 copy-start.15
  86.2 10.4 %copy-start.13 = (bf16[4,4,1,2,64,64]{5,0,4,3,1,2:T(4,128)(2,1)}, bf16[4,4,1,2,64,64]{5,0,4,3,1,2:T(4,128)(2,1)S(1)}, u32[]{:S(2)}) copy-start(bf16[4,4,1,2,64,64]{5,0,4,3,1,2:T(4,128)(2,1)S(1)} %get-tuple-element.967) | copy-start | bytes 786436 | tf_op jit(solution)/shard_map/while
  134.0 7.0 copy-start.7
  150.3 9.5 %copy-start = (f32[8,1152,64]{1,2,0:T(8,128)S(1)}, f32[8,1152,64]{1,2,0:T(8,128)}, u32[]{:S(2)}) copy-start(f32[8,1152,64]{1,2,0:T(8,128)} %fusion.129) | copy-start | bytes 7077892 | tf_op jit(solution)/shard_map/while
  248.0 10.4 %copy-start.13 = (bf16[4,4,1,2,64,64]{5,0,4,3,1,2:T(4,128)(2,1)}, bf16[4,4,1,2,64,64]{5,0,4,3,1,2:T(4,128)(2,1)S(1)}, u32[]{:S(2)}) copy-start(bf16[4,4,1,2,64,64]{5,0,4,3,1,2:T(4,128)(2,1)S(1)} %get-tuple-element.967) | copy-start | bytes 786436 | tf_op jit(solution)/shard_map/while
  312.0 9.5 %copy-start = (f32[8,1152,64]{1,2,0:T(8,128)S(1)}, f32[8,1152,64]{1,2,0:T(8,128)}, u32[]{:S(2)}) copy-start(f32[8,1152,64]{1,2,0:T(8,128)} %fusion.129) | copy-start | bytes 7077892 | tf_op jit(solution)/shard_map/while
  410.0 10.4 %copy-start.13 = (bf16[4,4,1,2,64,64]{5,0,4,3,1,2:T(4,128)(2,1)}, bf16[4,4,1,2,64,64]{5,0,4,3,1,2:T(4,128)(2,1)S(1)}, u32[]{:S(2)}) copy-start(bf16[4,4,1,2,64,64]{5,0,4,3,1,2:T(4,128)(2,1)S(1)} %get-tuple-element.967) | copy-start | bytes 786436 | tf_op jit(solution)/shard_map/while
  473.8 9.5 %copy-start = (f32[8,1152,64]{1,2,0:T(8,128)S(1)}, f32[8,1152,64]{1,2,0:T(8,128)}, u32[]{:S(2)}) copy-start(f32[8,1152,64]{1,2,0:T(8,128)} %fusion.129) | copy-start | bytes 7077892 | tf_op jit(solution)/shard_map/while
  571.7 10.4 %copy-start.13 = (bf16[4,4,1,2,64,64]{5,0,4,3,1,2:T(4,128)(2,1)}, bf16[4,4,1,2,64,64]{5,0,4,3,1,2:T(4,128)(2,1)S(1)}, u32[]{:S(2)}) copy-start(bf16[4,4,1,2,64,64]{5,0,4,3,1,2:T(4,128)(2,1)S(1)} %get-tuple-element.967) | copy-start | bytes 786436 | tf_op jit(solution)/shard_map/while
  635.7 9.5 %copy-start = (f32[8,1152,64]{1,2,0:T(8,128)S(1)}, f32[8,1152,64]{1,2,0:T(8,128)}, u32[]{:S(2)}) copy-start(f32[8,1152,64]{1,2,0:T(8,128)} %fusion.129) | copy-start | bytes 7077892 | tf_op jit(solution)/shard_map/while
  741.6 94.7 %collective-permute-start.2 = (f32[2,4,4,1,2,64,64]{6,5,1,0,4,3,2:T(8,128)}, f32[2,4,4,1,2,64,64]{6,5,1,0,4,3,2:T(8,128)S(1)}, u32[]{:S(2)}, u32[]{:S(2)}) collective-permute-start(f32[2,4,4,1,2,64,64]{6,5,1,0,4,3,2:T(8,128)} %get-tuple-element.768), channel_id=1, source_target_pairs={{0,1},{1,2},{2,3},{3,4},{4,5},{5,6},{6,7},{8,9},{9,10},{10,11},{11... | collective-permute-start | bytes 3145736 | tf_op jit(solution)/shard_map/ppermute | solution.py:22
  746.2 90.2 %collective-permute-start.3 = (f32[2,4,4,1,2,64,64]{6,5,1,0,4,3,2:T(8,128)}, f32[2,4,4,1,2,64,64]{6,5,1,0,4,3,2:T(8,128)}, u32[]{:S(2)}, u32[]{:S(2)}) collective-permute-start(f32[2,4,4,1,2,64,64]{6,5,1,0,4,3,2:T(8,128)} %get-tuple-element.769), channel_id=1, source_target_pairs={{1,0},{2,1},{3,2},{4,3},{5,4},{6,5},{7,6},{9,8},{10,9},{11,10},{12... | collective-permute-start | bytes 3145736 | tf_op jit(solution)/shard_map/ppermute | solution.py:23
  750.0 90.9 %all-to-all-start.4 = ((bf16[4,1,2,64,256]{4,3,2,1,0:T(8,128)(2,1)}), bf16[4,1,2,64,256]{4,3,2,1,0:T(8,128)(2,1)S(1)}, u32[]{:S(2)}, u32[]{:S(2)}) async-start(bf16[4,1,2,64,256]{4,3,2,1,0:T(8,128)(2,1)} %bitcast.18), calls=%async_computation.4 | async-start | bytes 524288 | tf_op jit(solution)/shard_map/all_to_all | solution.py:208
  840.8 9.4 %all-to-all-start.6 = ((bf16[4,1,2,64,256]{4,3,2,1,0:T(8,128)(2,1)}), bf16[4,1,2,64,256]{4,3,2,1,0:T(8,128)(2,1)S(1)}, u32[]{:S(2)}, u32[]{:S(2)}) async-start(bf16[4,1,2,64,256]{4,3,2,1,0:T(8,128)(2,1)} %bitcast.28), calls=%async_computation.6 | async-start | bytes 524288 | tf_op jit(solution)/shard_map/all_to_all | solution.py:212
  850.2 9.4 %all-to-all-start.5 = ((bf16[4,1,2,64,256]{4,3,2,1,0:T(8,128)(2,1)}), bf16[4,1,2,64,256]{4,3,2,1,0:T(8,128)(2,1)S(1)}, u32[]{:S(2)}, u32[]{:S(2)}) async-start(bf16[4,1,2,64,256]{4,3,2,1,0:T(8,128)(2,1)} %bitcast.23), calls=%async_computation.5 | async-start | bytes 524288 | tf_op jit(solution)/shard_map/all_to_all | solution.py:209
  (97 other events, 383.8 us)
where the time goes:
time: 870 us; the launch traced here: 861 us
  local copies, waits for them, and re-layouts  429 us (49%)
  matrix products  199 us (23%)
  waiting for transfers between devices  132 us (15%)
  other arithmetic  41.6 us (5%)
  starting transfers between devices  37.5 us (4%)
  loops' own time  20.9 us (2%)
    dot_general x4, matrix products, sweep_step(): jnp.einsum('abxyzpstf,wzs->wabxyzptf', deposits, selector, precision=lax....  176 us
    another operation x16, local copies, waits for them, and re-layouts, sweep_step(): jnp.stack([grad_key, grad_value])  109 us
    ppermute x2, waiting for transfers between devices, with_halo(): before = lax.ppermute(last, axis, up)  105 us
    slice x8, local copies, waits for them, and re-layouts, sweep_step(): by_offset[offset_z, :, :, :, :, :, pair_index]  64.9 us
    while x244, local copies, waits for them, and re-layouts  48.2 us
    reshape x36, local copies, waits for them, and re-layouts, sweep_step(): windows = jnp.stack(pieces, axis=5)  45.5 us
    gather x36, local copies, waits for them, and re-layouts, sweep_step(): chosen = jnp.take(plane, flat_z, axis=4)  38.7 us
    slice x4, local copies, waits for them, and re-layouts, sweep_step(): windows[1]  22.5 us
  transfers between devices with their start and end apart: 11, of which 8 were waited for; matrix products, arithmetic and copies ran while one was open for 2% of the time, Pallas kernels for 0%

commit v1 on v0

v1 whole, which is shorter than its diff:
```python
import functools
import math

import jax
import jax.numpy as jnp
from jax import lax
from jax.experimental import pallas as pl
from jax.experimental.pallas import tpu as pltpu
from jax.sharding import PartitionSpec as P

HD = 64
LANES = 128
NEG_FILL = -1e30
MESH = pl.DeviceIdType.MESH


def attention_kernel(
    cols, rows, groups, tokens, width, heads,
    q_ref, k_ref, v_ref, g_ref, dq_ref, dk_ref, dv_ref,
    qg, kv, acc, dq_out, kv_out, term_out, term_in,
    in_send, in_recv, halo_send, halo_recv, term_send, term_recv, out_send, out_recv,
):
    members = rows * cols
    scale = 1.0 / math.sqrt(HD)
    my_col = lax.axis_index("inline")
    my_y = lax.axis_index("xline")
    group = my_y // rows
    base_y = group * rows
    me_row = my_y - base_y
    me = me_row * cols + my_col
    has_above = group > 0
    has_below = group < groups - 1
    above = (my_col, jnp.maximum(my_y - rows, 0))
    below = (my_col, jnp.minimum(my_y + rows, groups * rows - 1))
    sides = ((has_above, above), (has_below, below))

    def chunk(ref, member):
        if width % LANES == 0:
            return ref.at[:, pl.ds(pl.multiple_of(member * width, LANES), width)]
        return ref.at[member]

    def remote(src, dst, send, recv, device):
        return pltpu.make_async_remote_copy(
            src_ref=src, dst_ref=dst, send_sem=send, recv_sem=recv,
            device_id=device, device_id_type=MESH,
        )

    def arrived(dst, sem):
        pltpu.make_async_copy(dst, dst, sem).wait()

    def partner(step):
        member = lax.rem(me + step, members)
        row = member // cols
        return member, (member - row * cols, base_y + row)

    barrier = pltpu.get_barrier_semaphore()
    for step in range(1, members):
        pl.semaphore_signal(barrier, inc=1, device_id=partner(step)[1], device_id_type=MESH)
    for present, device in sides:
        @pl.when(present)
        def _():
            pl.semaphore_signal(barrier, inc=1, device_id=device, device_id_type=MESH)
    pl.semaphore_wait(
        barrier, members - 1 + has_above.astype(jnp.int32) + has_below.astype(jnp.int32)
    )

    inputs = ((k_ref, 0), (v_ref, 1), (q_ref, 2), (g_ref, 3))

    def slot(array, row, col):
        return kv.at[array, row + 1, col] if array < 2 else qg.at[array - 2, row, col]

    def in_copy(ref, array, step):
        member, device = partner(step)
        return remote(
            chunk(ref, member), slot(array, me_row, my_col),
            in_send.at[array, step], in_recv.at[array, me], device,
        )

    for ref, array in inputs:
        for step in range(1, members):
            in_copy(ref, array, step).start()
        pltpu.make_async_copy(
            chunk(ref, me), slot(array, me_row, my_col), in_recv.at[array, me]
        ).start()

    acc[...] = jnp.zeros_like(acc)
    for side, (present, _) in enumerate(sides):
        @pl.when(jnp.logical_not(present))
        def _():
            for array in range(2):
                kv[array, side * (rows + 1)] = jnp.zeros_like(kv[array, 0])
                term_in[array, side] = jnp.zeros_like(term_in[array, side])

    def halo_copy(array, side, col):
        return remote(
            kv.at[array, 1 if side == 0 else rows, col],
            kv.at[array, rows + 1 if side == 0 else 0, col],
            halo_send.at[array, side, col], halo_recv.at[array, 1 - side, col],
            sides[side][1],
        )

    for array in range(2):
        for col in range(cols):
            for row in range(rows):
                arrived(slot(array, row, col), in_recv.at[array, row * cols + col])
            for side in range(2):
                @pl.when(sides[side][0])
                def _():
                    halo_copy(array, side, col).start()

    def await_halo(col):
        for array in range(2):
            for side in range(2):
                @pl.when(sides[side][0])
                def _():
                    arrived(kv.at[array, side * (rows + 1), col], halo_recv.at[array, side, col])

    lane = lax.broadcasted_iota(jnp.int32, (tokens, width), 1)

    def by_head(block, factor):
        wide = block.astype(jnp.float32) * factor
        if heads == 1:
            return wide.astype(jnp.bfloat16)
        return jnp.concatenate(
            [
                jnp.where((lane >= h * HD) & (lane < (h + 1) * HD), wide, 0.0).astype(jnp.bfloat16)
                for h in range(heads)
            ],
            axis=0,
        )

    def dot(a, b, contract):
        return lax.dot_general(
            a, b, ((contract[:1], contract[1:]), ((), ())), preferred_element_type=jnp.float32
        )

    def tile(row, col):
        first, last = max(col - 1, 0), min(col + 1, cols - 1)
        count = last - first + 1
        query = by_head(qg[0, row, col], scale)
        grad = by_head(qg[1, row, col], 1.0)
        key_rows = range(row, row + 3)

        def present(key_row):
            if key_row == 0:
                return has_above
            return has_below if key_row == rows + 1 else None

        def window(array, key_row):
            return kv[array, key_row, first : last + 1].reshape(count * tokens, width)

        scores = [dot(window(0, key_row), query, (1, 1)) for key_row in key_rows]
        peak = None
        for key_row, part in zip(key_rows, scores):
            part_peak = jnp.max(part, axis=0, keepdims=True)
            if present(key_row) is not None:
                part_peak = jnp.where(present(key_row), part_peak, NEG_FILL)
            peak = part_peak if peak is None else jnp.maximum(peak, part_peak)
        weights = []
        total = jnp.zeros_like(peak)
        for key_row, part in zip(key_rows, scores):
            shift = peak
            if present(key_row) is not None:
                shift = jnp.where(present(key_row), peak, -NEG_FILL)
            weights.append(jnp.exp(part - shift))
            total = total + jnp.sum(weights[-1], axis=0, keepdims=True)
        inverse = 1.0 / total
        row_dot = jnp.zeros_like(peak)
        dprobs = []
        for index, key_row in enumerate(key_rows):
            weights[index] = weights[index] * inverse
            dprobs.append(dot(window(1, key_row), grad, (1, 1)))
            row_dot = row_dot + jnp.sum(weights[index] * dprobs[index], axis=0, keepdims=True)
        turned = None
        for index, key_row in enumerate(key_rows):
            dscores = (weights[index] * (dprobs[index] - row_dot)).astype(jnp.bfloat16)
            low = weights[index].astype(jnp.bfloat16)
            block = (slice(None), slice(None))
            grad_key = dot(dscores, query, (1, 0)).reshape(count, tokens, width)
            acc[(0, key_row, slice(first, last + 1)) + block] += grad_key
            grad_value = dot(low, grad, (1, 0)).reshape(count, tokens, width)
            acc[(1, key_row, slice(first, last + 1)) + block] += grad_value
            term = dot(window(0, key_row), dscores, (0, 0))
            turned = term if turned is None else turned + term
        picked = jnp.concatenate(
            [turned[h * HD : (h + 1) * HD, h * tokens : (h + 1) * tokens] for h in range(heads)],
            axis=0,
        )
        dq_out[row, col] = (picked.T * scale).astype(jnp.bfloat16)

    outs = (dq_ref, dk_ref, dv_ref)

    def out_src(array, row, col):
        return dq_out.at[row, col] if array == 0 else kv_out.at[array - 1, row, col]

    def out_copy(array, row, col):
        return remote(
            out_src(array, row, col), chunk(outs[array], me),
            out_send.at[array, row, col], out_recv.at[array, me], (col, base_y + row),
        )

    def deliver(array, row, col):
        own = me == row * cols + col

        @pl.when(own)
        def _():
            pltpu.make_async_copy(
                out_src(array, row, col), chunk(outs[array], me), out_recv.at[array, me]
            ).start()

        @pl.when(jnp.logical_not(own))
        def _():
            out_copy(array, row, col).start()

    def term_copy(array, side, col):
        return remote(
            term_out.at[array, side, col], term_in.at[array, 1 - side, col],
            term_send.at[array, side, col], term_recv.at[array, 1 - side, col],
            sides[side][1],
        )

    def send_terms(col):
        for array in range(2):
            for side in range(2):
                @pl.when(sides[side][0])
                def _():
                    term_out[array, side, col] = acc[array, side * (rows + 1), col].astype(
                        jnp.bfloat16
                    )
                    term_copy(array, side, col).start()

    def finish(col):
        for array in range(2):
            for side in range(2):
                @pl.when(sides[side][0])
                def _():
                    arrived(term_in.at[array, side, col], term_recv.at[array, side, col])
            for row in range(rows):
                total = acc[array, row + 1, col]
                if row == 0:
                    total = total + term_in[array, 0, col].astype(jnp.float32)
                if row == rows - 1:
                    total = total + term_in[array, 1, col].astype(jnp.float32)
                kv_out[array, row, col] = total.astype(jnp.bfloat16)
                deliver(array + 1, row, col)

    await_halo(0)
    for col in range(cols):
        if col + 1 < cols:
            await_halo(col + 1)
        for row in range(rows):
            for array in (2, 3):
                arrived(slot(array, row, col), in_recv.at[array, row * cols + col])
            tile(row, col)
            deliver(0, row, col)
        if col >= 1:
            send_terms(col - 1)
        if col >= 2:
            finish(col - 2)
    send_terms(cols - 1)
    for col in range(max(cols - 2, 0), cols):
        finish(col)

    for ref, array in inputs:
        for step in range(1, members):
            in_copy(ref, array, step).wait_send()
    for array in range(2):
        for side in range(2):
            for col in range(cols):
                @pl.when(sides[side][0])
                def _():
                    halo_copy(array, side, col).wait_send()
                    term_copy(array, side, col).wait_send()
    for array in range(3):
        for row in range(rows):
            for col in range(cols):
                @pl.when(me != row * cols + col)
                def _():
                    out_copy(array, row, col).wait_send()
        for member in range(members):
            arrived(chunk(outs[array], member), out_recv.at[array, member])


def shards(rows, cols, groups, queries, keys, values, grad_out):
    shape = queries.shape
    tokens, full = shape[2] * shape[3], shape[4]
    members = rows * cols
    width = full // members
    heads = width // HD

    def pack(array):
        array = array.reshape(tokens, full)
        if width % LANES == 0:
            return array
        return array.reshape(tokens, members, width).transpose(1, 0, 2)

    def unpack(array):
        if width % LANES:
            array = array.transpose(1, 0, 2)
        return array.reshape(shape)

    packed = (tokens, full) if width % LANES == 0 else (members, tokens, width)
    low, wide = jnp.bfloat16, jnp.float32
    dma = pltpu.SemaphoreType.DMA
    outputs = pl.pallas_call(
        functools.partial(attention_kernel, cols, rows, groups, tokens, width, heads),
        out_shape=[jax.ShapeDtypeStruct(packed, low)] * 3,
        in_specs=[pl.BlockSpec(memory_space=pl.ANY)] * 4,
        out_specs=[pl.BlockSpec(memory_space=pl.ANY)] * 3,
        scratch_shapes=[
            pltpu.VMEM((2, rows, cols, tokens, width), low),
            pltpu.VMEM((2, rows + 2, cols, tokens, width), low),
            pltpu.VMEM((2, rows + 2, cols, tokens, width), wide),
            pltpu.VMEM((rows, cols, tokens, width), low),
            pltpu.VMEM((2, rows, cols, tokens, width), low),
            pltpu.VMEM((2, 2, cols, tokens, width), low),
            pltpu.VMEM((2, 2, cols, tokens, width), low),
            dma((4, members)),
            dma((4, members)),
            dma((2, 2, cols)),
            dma((2, 2, cols)),
            dma((2, 2, cols)),
            dma((2, 2, cols)),
            dma((3, rows, cols)),
            dma((3, members)),
        ],
        compiler_params=pltpu.CompilerParams(
            collective_id=0, has_side_effects=True, vmem_limit_bytes=48 * 1024 * 1024
        ),
    )(pack(queries), pack(keys), pack(values), pack(grad_out))
    return tuple(unpack(array) for array in outputs)


def solution(mesh):
    cols, lines = mesh.shape["inline"], mesh.shape["xline"]
    spec = P("inline", "xline", None, None, None)

    def body(queries, keys, values, grad_out):
        heads = queries.shape[4] // HD
        rows = 2 if heads % (2 * cols) == 0 and lines % 2 == 0 else 1
        return shards(rows, cols, lines // rows, queries, keys, values, grad_out)

    return jax.shard_map(
        body, mesh=mesh, in_specs=(spec,) * 4, out_specs=(spec,) * 3, check_vma=False
    )
```

time: 870 us -> 44.2 us (0.05); the launches traced: 861 us -> 43.9 us
  local copies, waits for them, and re-layouts: 429 us -> 5.9 us
  matrix products: 199 us -> 0 us
  waiting for transfers between devices: 132 us -> 0 us
  other arithmetic: 41.6 us -> 0 us
  starting transfers between devices: 37.5 us -> 0 us
  Pallas kernels: 0 us -> 37.4 us
  loops' own time: 20.9 us -> 0 us
    dot_general x28 -> x0, matrix products: 199 us -> none  [the longest x4 176 us: sweep_step(): jnp.einsum('abxyzpstf,wzs->wabxyzptf', deposits, selector, precision=lax....]
    another operation x44 -> x0, local copies, waits for them, and re-layouts: 125 us -> none  [the longest x16 109 us: sweep_step(): jnp.stack([grad_key, grad_value])]
    slice x17 -> x0, local copies, waits for them, and re-layouts: 106 us -> none  [the longest x8 64.9 us: sweep_step(): by_offset[offset_z, :, :, :, :, :, pair_index]]
    ppermute x4 -> x0, waiting for transfers between devices: 105 us -> none  [the longest x2 105 us: with_halo(): before = lax.ppermute(last, axis, up)]
    reshape x43 -> x0, local copies, waits for them, and re-layouts: 49.6 us -> none  [the longest x36 45.5 us: sweep_step(): windows = jnp.stack(pieces, axis=5)]
    while x244 -> x0, local copies, waits for them, and re-layouts: 48.2 us -> none
    gather x36 -> x0, local copies, waits for them, and re-layouts: 38.7 us -> none  [sweep_step(): chosen = jnp.take(plane, flat_z, axis=4)]
    pallas_call x0 -> x1, Pallas kernels: none -> 37.4 us  [shards(): pl.pallas_call(functools.partial(attention_kernel, cols, rows, groups, to...]
  transfers between devices with their start and end apart: 11 -> 0, of which waited for: 8 -> 0; matrix products, arithmetic and copies ran while one was open for 2% -> 0% of each run, Pallas kernels for 0% -> 0%
where the time goes in v1:
time: 44.2 us; the launch traced here: 43.9 us
  Pallas kernels  37.4 us (85%)
  local copies, waits for them, and re-layouts  5.9 us (13%)
  between operations  0.65 us (1%)
    pallas_call x1, Pallas kernels, shards(): pl.pallas_call(functools.partial(attention_kernel, cols, rows, groups, to...  37.4 us
    unnamed x11, local copies, waits for them, and re-layouts  5.9 us

profile of v1, /device:TPU:0, one launch (start us, length us, event | category | flops | bytes accessed | tf_op | source)
XLA Modules:
  0.0 43.9 jit_solution(2544466101527476299)
XLA Ops:
  0.6 0.0 copy-start
  0.6 0.9 %copy-done = bf16[1,1,2,64,1024]{4,3,2,1,0:T(8,128)(2,1)S(1)} copy-done((bf16[1,1,2,64,1024]{4,3,2,1,0:T(8,128)(2,1)S(1)}, bf16[1,1,2,64,1024]{4,3,2,1,0:T(8,128)(2,1)}, u32[]{:S(2)}) %copy-start) | copy-done | bytes 262168
  1.6 0.0 copy-start.1
  1.6 0.9 %copy-done.1 = bf16[1,1,2,64,1024]{4,3,2,1,0:T(8,128)(2,1)S(1)} copy-done((bf16[1,1,2,64,1024]{4,3,2,1,0:T(8,128)(2,1)S(1)}, bf16[1,1,2,64,1024]{4,3,2,1,0:T(8,128)(2,1)}, u32[]{:S(2)}) %copy-start.1) | copy-done | bytes 262168
  2.5 0.0 copy-start.2
  2.5 0.9 %copy-done.2 = bf16[1,1,2,64,1024]{4,3,2,1,0:T(8,128)(2,1)S(1)} copy-done((bf16[1,1,2,64,1024]{4,3,2,1,0:T(8,128)(2,1)S(1)}, bf16[1,1,2,64,1024]{4,3,2,1,0:T(8,128)(2,1)}, u32[]{:S(2)}) %copy-start.2) | copy-done | bytes 262168
  3.5 0.0 copy-start.3
  3.5 0.9 %copy-done.3 = bf16[1,1,2,64,1024]{4,3,2,1,0:T(8,128)(2,1)S(1)} copy-done((bf16[1,1,2,64,1024]{4,3,2,1,0:T(8,128)(2,1)S(1)}, bf16[1,1,2,64,1024]{4,3,2,1,0:T(8,128)(2,1)}, u32[]{:S(2)}) %copy-start.3) | copy-done | bytes 262168
  4.4 37.4 %shard_map.67 = (bf16[128,1024]{1,0:T(8,128)(2,1)S(1)}, bf16[128,1024]{1,0:T(8,128)(2,1)S(1)}, bf16[128,1024]{1,0:T(8,128)(2,1)S(1)}) custom-call(bf16[128,1024]{1,0:T(8,128)(2,1)S(1)} %bitcast.10, bf16[128,1024]{1,0:T(8,128)(2,1)S(1)} %bitcast.11, bf16[128,1024]{1,0:T(8,128)(2,1)S(1)} %bitcast.12, bf16[128,1024]{1,0:T(8,128)(2,1)S(1)} %bitcast.13), custom_call_target="tpu_custom_call" | custom-call | tf_op jit(solution)/shard_map/pallas_call | solution.py:305
  41.8 0.7 %copy.10 = bf16[1,1,2,64,1024]{4,3,2,1,0:T(8,128)(2,1)} copy(bf16[1,1,2,64,1024]{4,3,2,1,0:T(8,128)(2,1)S(1)} %bitcast.9) | data formatting | bytes 524288
  42.5 0.7 %copy.11 = bf16[1,1,2,64,1024]{4,3,2,1,0:T(8,128)(2,1)} copy(bf16[1,1,2,64,1024]{4,3,2,1,0:T(8,128)(2,1)S(1)} %bitcast.8) | data formatting | bytes 524288
  43.2 0.7 %copy.12 = bf16[1,1,2,64,1024]{4,3,2,1,0:T(8,128)(2,1)} copy(bf16[1,1,2,64,1024]{4,3,2,1,0:T(8,128)(2,1)S(1)} %bitcast.7) | data formatting | bytes 524288
Async XLA Ops:
  0.6 1.0 %copy-start = (bf16[1,1,2,64,1024]{4,3,2,1,0:T(8,128)(2,1)S(1)}, bf16[1,1,2,64,1024]{4,3,2,1,0:T(8,128)(2,1)}, u32[]{:S(2)}) copy-start(bf16[1,1,2,64,1024]{4,3,2,1,0:T(8,128)(2,1)} %param.4) | copy-start | bytes 786436
  1.6 0.9 %copy-start.1 = (bf16[1,1,2,64,1024]{4,3,2,1,0:T(8,128)(2,1)S(1)}, bf16[1,1,2,64,1024]{4,3,2,1,0:T(8,128)(2,1)}, u32[]{:S(2)}) copy-start(bf16[1,1,2,64,1024]{4,3,2,1,0:T(8,128)(2,1)} %param.5) | copy-start | bytes 786436
  2.5 0.9 %copy-start.2 = (bf16[1,1,2,64,1024]{4,3,2,1,0:T(8,128)(2,1)S(1)}, bf16[1,1,2,64,1024]{4,3,2,1,0:T(8,128)(2,1)}, u32[]{:S(2)}) copy-start(bf16[1,1,2,64,1024]{4,3,2,1,0:T(8,128)(2,1)} %param.6) | copy-start | bytes 786436
  3.5 0.9 %copy-start.3 = (bf16[1,1,2,64,1024]{4,3,2,1,0:T(8,128)(2,1)S(1)}, bf16[1,1,2,64,1024]{4,3,2,1,0:T(8,128)(2,1)}, u32[]{:S(2)}) copy-start(bf16[1,1,2,64,1024]{4,3,2,1,0:T(8,128)(2,1)} %param.7) | copy-start | bytes 786436

commit v2 on v1

--- a/solution.py
+++ b/solution.py
@@ -17,7 +17,7 @@
 def attention_kernel(
     cols, rows, groups, tokens, width, heads,
     q_ref, k_ref, v_ref, g_ref, dq_ref, dk_ref, dv_ref,
-    qg, kv, acc, dq_out, kv_out, term_out, term_in,
+    qg, kv, acc, weights, query_heads, grad_heads, dq_out, kv_out, term_out, term_in,
     in_send, in_recv, halo_send, halo_recv, term_send, term_recv, out_send, out_recv,
 ):
     members = rows * cols
@@ -64,7 +64,7 @@
         barrier, members - 1 + has_above.astype(jnp.int32) + has_below.astype(jnp.int32)
     )
 
-    inputs = ((k_ref, 0), (v_ref, 1), (q_ref, 2), (g_ref, 3))
+    inputs = ((k_ref, 0), (q_ref, 2), (v_ref, 1), (g_ref, 3))
 
     def slot(array, row, col):
         return kv.at[array, row + 1, col] if array < 2 else qg.at[array - 2, row, col]
@@ -76,12 +76,16 @@
             in_send.at[array, step], in_recv.at[array, me], device,
         )
 
-    for ref, array in inputs:
+    def spread(index):
+        ref, array = inputs[index]
         for step in range(1, members):
             in_copy(ref, array, step).start()
         pltpu.make_async_copy(
             chunk(ref, me), slot(array, me_row, my_col), in_recv.at[array, me]
         ).start()
+
+    spread(0)
+    spread(1)
 
     acc[...] = jnp.zeros_like(acc)
     for side, (present, _) in enumerate(sides):
@@ -99,7 +103,7 @@
             sides[side][1],
         )
 
-    for array in range(2):
+    def forward(array):
         for col in range(cols):
             for row in range(rows):
                 arrived(slot(array, row, col), in_recv.at[array, row * cols + col])
@@ -108,12 +112,13 @@
                 def _():
                     halo_copy(array, side, col).start()
 
-    def await_halo(col):
-        for array in range(2):
-            for side in range(2):
-                @pl.when(sides[side][0])
-                def _():
-                    arrived(kv.at[array, side * (rows + 1), col], halo_recv.at[array, side, col])
+    def await_halo(array, col):
+        if col >= cols:
+            return
+        for side in range(2):
+            @pl.when(sides[side][0])
+            def _():
+                arrived(kv.at[array, side * (rows + 1), col], halo_recv.at[array, side, col])
 
     lane = lax.broadcasted_iota(jnp.int32, (tokens, width), 1)
 
@@ -134,53 +139,70 @@
             a, b, ((contract[:1], contract[1:]), ((), ())), preferred_element_type=jnp.float32
         )
 
-    def tile(row, col):
+    def span(col):
         first, last = max(col - 1, 0), min(col + 1, cols - 1)
-        count = last - first + 1
+        return first, last - first + 1
+
+    def window(array, key_row, col):
+        first, count = span(col)
+        return kv[array, key_row, first : first + count].reshape(count * tokens, width)
+
+    def present(key_row):
+        if key_row == 0:
+            return has_above
+        return has_below if key_row == rows + 1 else None
+
+    def softmax(row, col):
+        _, count = span(col)
         query = by_head(qg[0, row, col], scale)
-        grad = by_head(qg[1, row, col], 1.0)
+        query_heads[row, col] = query
         key_rows = range(row, row + 3)
-
-        def present(key_row):
-            if key_row == 0:
-                return has_above
-            return has_below if key_row == rows + 1 else None
-
-        def window(array, key_row):
-            return kv[array, key_row, first : last + 1].reshape(count * tokens, width)
-
-        scores = [dot(window(0, key_row), query, (1, 1)) for key_row in key_rows]
+        scores = [dot(window(0, key_row, col), query, (1, 1)) for key_row in key_rows]
         peak = None
         for key_row, part in zip(key_rows, scores):
             part_peak = jnp.max(part, axis=0, keepdims=True)
             if present(key_row) is not None:
                 part_peak = jnp.where(present(key_row), part_peak, NEG_FILL)
             peak = part_peak if peak is None else jnp.maximum(peak, part_peak)
-        weights = []
+        terms = []
         total = jnp.zeros_like(peak)
         for key_row, part in zip(key_rows, scores):
             shift = peak
             if present(key_row) is not None:
                 shift = jnp.where(present(key_row), peak, -NEG_FILL)
-            weights.append(jnp.exp(part - shift))
-            total = total + jnp.sum(weights[-1], axis=0, keepdims=True)
+            terms.append(jnp.exp(part - shift))
+            total = total + jnp.sum(terms[-1], axis=0, keepdims=True)
         inverse = 1.0 / total
-        row_dot = jnp.zeros_like(peak)
+        for index in range(3):
+            weights[row, col, index, : count * tokens] = terms[index] * inverse
+
+    def value_gradient(row, col):
+        first, count = span(col)
+        grad = by_head(qg[1, row, col], 1.0)
+        grad_heads[row, col] = grad
+        for index in range(3):
+            low = weights[row, col, index, : count * tokens].astype(jnp.bfloat16)
+            term = dot(low, grad, (1, 0)).reshape(count, tokens, width)
+            acc[1, row + index, first : first + count] += term
+
+    def gradients(row, col):
+        first, count = span(col)
+        query = query_heads[row, col]
+        grad = grad_heads[row, col]
+        row_dot = None
         dprobs = []
-        for index, key_row in enumerate(key_rows):
-            weights[index] = weights[index] * inverse
-            dprobs.append(dot(window(1, key_row), grad, (1, 1)))
-            row_dot = row_dot + jnp.sum(weights[index] * dprobs[index], axis=0, keepdims=True)
+        probs = [weights[row, col, index, : count * tokens] for index in range(3)]
+        for index in range(3):
+            dprobs.append(dot(window(1, row + index, col), grad, (1, 1)))
+            part_dot = jnp.sum(probs[index] * dprobs[index], axis=0, keepdims=True)
+            row_dot = part_dot if row_dot is None else row_dot + part_dot
         turned = None
-        for index, key_row in enumerate(key_rows):
-            dscores = (weights[index] * (dprobs[index] - row_dot)).astype(jnp.bfloat16)
-            low = weights[index].astype(jnp.bfloat16)
-            block = (slice(None), slice(None))
+        for index in range(3):
+            key_row = row + index
+            dscores = (probs[index] * (dprobs[index] - row_dot)).astype(jnp.bfloat16)
             grad_key = dot(dscores, query, (1, 0)).reshape(count, tokens, width)
-            acc[(0, key_row, slice(first, last + 1)) + block] += grad_key
-            grad_value = dot(low, grad, (1, 0)).reshape(count, tokens, width)
-            acc[(1, key_row, slice(first, last + 1)) + block] += grad_value
-            term = dot(window(0, key_row), dscores, (0, 0))
+            acc[0, key_row, first : first + count] += grad_key
+            term = dot(window(0, key_row, col), dscores, (0, 0))
             turned = term if turned is None else turned + term
         picked = jnp.concatenate(
             [turned[h * HD : (h + 1) * HD, h * tokens : (h + 1) * tokens] for h in range(heads)],
@@ -219,47 +241,70 @@
             sides[side][1],
         )
 
-    def send_terms(col):
-        for array in range(2):
-            for side in range(2):
-                @pl.when(sides[side][0])
-                def _():
-                    term_out[array, side, col] = acc[array, side * (rows + 1), col].astype(
-                        jnp.bfloat16
-                    )
-                    term_copy(array, side, col).start()
-
-    def finish(col):
-        for array in range(2):
-            for side in range(2):
-                @pl.when(sides[side][0])
-                def _():
-                    arrived(term_in.at[array, side, col], term_recv.at[array, side, col])
-            for row in range(rows):
-                total = acc[array, row + 1, col]
-                if row == 0:
-                    total = total + term_in[array, 0, col].astype(jnp.float32)
-                if row == rows - 1:
-                    total = total + term_in[array, 1, col].astype(jnp.float32)
-                kv_out[array, row, col] = total.astype(jnp.bfloat16)
-                deliver(array + 1, row, col)
-
-    await_halo(0)
+    def send_terms(array, col):
+        for side in range(2):
+            @pl.when(sides[side][0])
+            def _():
+                term_out[array, side, col] = acc[array, side * (rows + 1), col].astype(
+                    jnp.bfloat16
+                )
+                term_copy(array, side, col).start()
+
+    def finish(array, col):
+        for side in range(2):
+            @pl.when(sides[side][0])
+            def _():
+                arrived(term_in.at[array, side, col], term_recv.at[array, side, col])
+        for row in range(rows):
+            total = acc[array, row + 1, col]
+            if row == 0:
+                total = total + term_in[array, 0, col].astype(jnp.float32)
+            if row == rows - 1:
+                total = total + term_in[array, 1, col].astype(jnp.float32)
+            kv_out[array, row, col] = total.astype(jnp.bfloat16)
+            deliver(array + 1, row, col)
+
+    def await_input(array, row, col):
+        arrived(slot(array, row, col), in_recv.at[array, row * cols + col])
+
+    def await_array(array):
+        for row in range(rows):
+            for col in range(cols):
+                await_input(array, row, col)
+
+    forward(0)
+    spread(2)
+    await_array(2)
+    spread(3)
+    await_halo(0, 0)
     for col in range(cols):
-        if col + 1 < cols:
-            await_halo(col + 1)
-        for row in range(rows):
-            for array in (2, 3):
-                arrived(slot(array, row, col), in_recv.at[array, row * cols + col])
-            tile(row, col)
+        await_halo(0, col + 1)
+        for row in range(rows):
+            softmax(row, col)
+    forward(1)
+    await_array(3)
+    for col in range(cols):
+        for row in range(rows):
+            value_gradient(row, col)
+        if col >= 1:
+            send_terms(1, col - 1)
+    send_terms(1, cols - 1)
+    await_halo(1, 0)
+    for col in range(cols):
+        await_halo(1, col + 1)
+        for row in range(rows):
+            gradients(row, col)
+        if col >= 1:
+            send_terms(0, col - 1)
+        if col == cols - 1:
+            send_terms(0, col)
+        finish(1, col)
+        if col >= 2:
+            finish(0, col - 2)
+        for row in range(rows):
             deliver(0, row, col)
-        if col >= 1:
-            send_terms(col - 1)
-        if col >= 2:
-            finish(col - 2)
-    send_terms(cols - 1)
     for col in range(max(cols - 2, 0), cols):
-        finish(col)
+        finish(0, col)
 
     for ref, array in inputs:
         for step in range(1, members):
@@ -281,6 +326,17 @@
             arrived(chunk(outs[array], member), out_recv.at[array, member])
 
 
+def flush_kernel(a_ref, b_ref, c_ref, a_out, b_out, c_out, sems):
+    copies = [
+        pltpu.make_async_copy(src, dst, sems.at[index])
+        for index, (src, dst) in enumerate(((a_ref, a_out), (b_ref, b_out), (c_ref, c_out)))
+    ]
+    for copy in copies:
+        copy.start()
+    for copy in copies:
+        copy.wait()
+
+
 def shards(rows, cols, groups, queries, keys, values, grad_out):
     shape = queries.shape
     tokens, full = shape[2] * shape[3], shape[4]
@@ -306,11 +362,14 @@
         functools.partial(attention_kernel, cols, rows, groups, tokens, width, heads),
         out_shape=[jax.ShapeDtypeStruct(packed, low)] * 3,
         in_specs=[pl.BlockSpec(memory_space=pl.ANY)] * 4,
-        out_specs=[pl.BlockSpec(memory_space=pl.ANY)] * 3,
+        out_specs=[pl.BlockSpec(memory_space=pltpu.MemorySpace.VMEM)] * 3,
         scratch_shapes=[
             pltpu.VMEM((2, rows, cols, tokens, width), low),
             pltpu.VMEM((2, rows + 2, cols, tokens, width), low),
             pltpu.VMEM((2, rows + 2, cols, tokens, width), wide),
+            pltpu.VMEM((rows, cols, 3, 3 * tokens, heads * tokens), wide),
+            pltpu.VMEM((rows, cols, heads * tokens, width), low),
+            pltpu.VMEM((rows, cols, heads * tokens, width), low),
             pltpu.VMEM((rows, cols, tokens, width), low),
             pltpu.VMEM((2, rows, cols, tokens, width), low),
             pltpu.VMEM((2, 2, cols, tokens, width), low),
@@ -325,9 +384,17 @@
             dma((3, members)),
         ],
         compiler_params=pltpu.CompilerParams(
-            collective_id=0, has_side_effects=True, vmem_limit_bytes=48 * 1024 * 1024
+            collective_id=0, has_side_effects=True, vmem_limit_bytes=62 * 1024 * 1024
         ),
     )(pack(queries), pack(keys), pack(values), pack(grad_out))
+    outputs = pl.pallas_call(
+        flush_kernel,
+        out_shape=[jax.ShapeDtypeStruct(packed, low)] * 3,
+        in_specs=[pl.BlockSpec(memory_space=pltpu.MemorySpace.VMEM)] * 3,
+        out_specs=[pl.BlockSpec(memory_space=pl.ANY)] * 3,
+        scratch_shapes=[dma((3,))],
+        compiler_params=pltpu.CompilerParams(vmem_limit_bytes=62 * 1024 * 1024),
+    )(*outputs)
     return tuple(unpack(array) for array in outputs)
 
 

time: 44.2 us -> 39.4 us (0.89)
  local copies, waits for them, and re-layouts: 5.9 us -> 0 us
  Pallas kernels: 37.4 us -> 38.5 us
    unnamed x11 -> x0, local copies, waits for them, and re-layouts: 5.9 us -> none
    pallas_call x0 -> x1, Pallas kernels: none -> 2.01 us  [shards(): pl.pallas_call(flush_kernel, out_shape=[jax.ShapeDtypeStruct(packed, low)...]
    pallas_call x1, Pallas kernels: 37.4 us -> 36.5 us  [shards(): pl.pallas_call(functools.partial(attention_kernel, cols, rows, groups, to...]
where the time goes in v2:
time: 39.4 us; the launch traced here: 39.2 us
  Pallas kernels  38.5 us (98%)
  between operations  0.64 us (2%)
    pallas_call x1, Pallas kernels, shards(): pl.pallas_call(functools.partial(attention_kernel, cols, rows, groups, to...  36.5 us
    pallas_call x1, Pallas kernels, shards(): pl.pallas_call(flush_kernel, out_shape=[jax.ShapeDtypeStruct(packed, low)...  2.01 us

profile of v2, /device:TPU:0, one launch (start us, length us, event | category | flops | bytes accessed | tf_op | source)
XLA Modules:
  0.0 39.2 jit_solution(5567309479909998839)
XLA Ops:
  0.6 36.5 %shard_map.67 = (bf16[128,1024]{1,0:T(8,128)(2,1)}, bf16[128,1024]{1,0:T(8,128)(2,1)}, bf16[128,1024]{1,0:T(8,128)(2,1)}) custom-call(bf16[128,1024]{1,0:T(8,128)(2,1)} %bitcast.7, bf16[128,1024]{1,0:T(8,128)(2,1)} %bitcast.8, bf16[128,1024]{1,0:T(8,128)(2,1)} %bitcast.9, bf16[128,1024]{1,0:T(8,128)(2,1)} %bitcast.10), custom_call_target="tpu_custom_call" | custom-call | tf_op jit(solution)/shard_map/pallas_call | solution.py:361
  37.2 2.0 %shard_map.68 = (bf16[128,1024]{1,0:T(8,128)(2,1)}, bf16[128,1024]{1,0:T(8,128)(2,1)}, bf16[128,1024]{1,0:T(8,128)(2,1)}) custom-call(bf16[128,1024]{1,0:T(8,128)(2,1)} %get-tuple-element.9.a_ref, bf16[128,1024]{1,0:T(8,128)(2,1)} %get-tuple-element.10.b_ref, bf16[128,1024]{1,0:T(8,128)(2,1)} %get-tuple-element.11.c_ref), custom_call_target="tpu_custom_call" | custom-call | tf_op jit(solution)/shard_map/pallas_call | solution.py:390
